TPU v7x, 128 devices: a whole 4x4x4 slice. The times are simulated.
128 devices in a mesh: ia: 2 (over z_hi), ja: 8 (over x, core), ka: 8 (over y, z_lo).
Axes of the slice: x: 4, y: 4, z: 4 (z_hi: 2, z_lo: 2; z = z_hi * 2 + z_lo), core: 2. Of those that a mesh axis runs over, the one named last changes fastest.
Arguments:
- hidden_act: bfloat16 [768, 26624], P(('ia', 'ka'), 'ja'), may hold values from -6 to 6
- w_down: bfloat16 [26624, 16384], P('ja', ('ia', 'ka')), may hold values from -0.0390625 to 0.0390625
- w_out: bfloat16 [16384, 16384], P(('ia', 'ka'), 'ja'), may hold values from -0.046875 to 0.046875
- head_grad: bfloat16 [768, 16384], P(('ia', 'ka'), 'ja'), may hold values from -6 to 6
- token_ratio: float32 [768], P(('ia', 'ka')), may hold values from -4 to 4
- pair_slot: int32 [768], P(('ia', 'ka')), may hold values from 0 to 15
- segment_id: int32 [768], P(('ia', 'ka')), may hold values from 0 to 191, never falling along the last dimension, each value on 1 to 16 neighbouring positions
Outputs:
- projected: bfloat16 [768, 16384], P(('ia', 'ka'), 'ja')
- grad_hidden: bfloat16 [768, 26624], P(('ia', 'ka'), 'ja')
- grad_down: bfloat16 [26624, 16384], P('ja', ('ia', 'ka'))
- grad_out: bfloat16 [16384, 16384], P(('ia', 'ka'), 'ja')
All inputs are finite; a program needn't handle non-finite values.
Results may differ from a plain program's by a relative error of at most 0.0058.
Values may be sent and summed in bfloat16 or wider, within the bound.
A program may use at most 128 MiB of HBM per device.

v0:
```python
import jax
import jax.numpy as jnp
from jax import lax
from jax.sharding import PartitionSpec as P

PAIRS = 8
beta_scale = 0.5


def gather_rows(block):
    return lax.all_gather(block, ("ia", "ka"), axis=0, tiled=True)


def scatter_rows(term, local_rows):
    return lax.psum_scatter(
        term(jnp.int32(0), local_rows * lax.axis_size(("ia", "ka"))),
        ("ia", "ka"),
        scatter_dimension=0,
        tiled=True,
    )


def summed_middle(term, total_rows):
    shares = lax.psum_scatter(
        term(jnp.int32(0), total_rows // lax.axis_size("ja") * lax.axis_size("ja")),
        "ja",
        scatter_dimension=0,
        tiled=True,
    ).astype(jnp.bfloat16)
    return lax.all_gather(shares, "ja", axis=0, tiled=True)


def contract_last(left, right):
    return lax.dot_general(
        left, right, (((1,), (1,)), ((), ())), preferred_element_type=jnp.float32
    )


def contract_first(left, right):
    return lax.dot_general(
        left, right, (((0,), (0,)), ((), ())), preferred_element_type=jnp.float32
    )


def local(hidden_act, w_down, w_out, head_grad, token_ratio, pair_slot, segment_id):
    local_rows = hidden_act.shape[0]
    total_rows = local_rows * lax.axis_size("ia") * lax.axis_size("ka")
    full_hidden = gather_rows(hidden_act)

    def down_term(start, count):
        return jnp.dot(full_hidden, w_down, preferred_element_type=jnp.float32)

    down_full = summed_middle(down_term, total_rows)

    def out_term(start, count):
        return jnp.dot(down_full, w_out, preferred_element_type=jnp.float32)

    projected = scatter_rows(out_term, local_rows).astype(jnp.bfloat16)
    masked = (segment_id % 2).astype(jnp.float32)
    signed = masked * (1 - 2 * (pair_slot % 2)).astype(jnp.float32)
    onehot = ((pair_slot // 2)[:, None] == jnp.arange(PAIRS, dtype=jnp.int32)[None, :]).astype(
        jnp.float32
    )
    local_margin = jnp.dot(signed * token_ratio, onehot, precision=lax.Precision.HIGHEST)
    margin = lax.psum(local_margin, ("ia", "ka"))
    pair_weight = -beta_scale * jax.nn.sigmoid(-beta_scale * margin)
    coef = jnp.dot(onehot, pair_weight, precision=lax.Precision.HIGHEST) * signed
    cotangent = (coef[:, None] * head_grad.astype(jnp.float32)).astype(jnp.bfloat16)
    full_cotangent = gather_rows(cotangent)

    def back_term(start, count):
        return contract_last(full_cotangent, w_out)

    grad_mid = summed_middle(back_term, total_rows)
    grad_out = contract_first(down_full, full_cotangent).astype(jnp.bfloat16)

    def hidden_term(start, count):
        return contract_last(grad_mid, w_down)

    grad_hidden = scatter_rows(hidden_term, local_rows).astype(jnp.bfloat16)
    grad_down = contract_first(full_hidden, grad_mid).astype(jnp.bfloat16)
    return (projected, grad_hidden, grad_down, grad_out)


def solution(mesh):
    placed = (
        P(("ia", "ka"), "ja"),
        P("ja", ("ia", "ka")),
        P(("ia", "ka"), "ja"),
        P(("ia", "ka"), "ja"),
        P(("ia", "ka")),
        P(("ia", "ka")),
        P(("ia", "ka")),
    )
    return jax.shard_map(
        local,
        mesh=mesh,
        in_specs=placed,
        out_specs=(
            P(("ia", "ka"), "ja"),
            P(("ia", "ka"), "ja"),
            P("ja", ("ia", "ka")),
            P(("ia", "ka"), "ja"),
        ),
        check_vma=False,
    )
```

profile of v0, /device:TPU:9, one launch (start us, length us, event | category | flops | bytes accessed | tf_op | source)
XLA Modules:
  0.0 708.8 jit_solution(12141324303579329130)
XLA Ops:
  7.2 0.0 all-gather.5.cloned.1.call-start
  7.2 0.7 all-gather.5.cloned.1.call-update
  7.9 0.0 all-gather.9.cloned.1.call-start
  7.9 0.7 and_select_fusion.2
  8.6 0.7 fusion.5
  9.3 0.8 convolution_bitcast_fusion.1
  10.1 33.9 %psum.7 = f32[8]{0:T(128)S(1)} all-reduce(f32[8]{0:T(128)S(1)} %convolution_bitcast_fusion.1), channel_id=1, replica_groups=mesh['ia'=2,'ja'=8,'ka'=8] {'ia','ka'}, use_global_device_ids=true, to_apply=%region_2.3 | all-reduce | flops 8 | bytes 64 | tf_op jit(solution)/shard_map/psum | solution.py:65
  44.0 0.2 fusion.1
  44.2 1.7 multiply_convert_fusion
  45.9 0.0 all-gather.9.cloned.1.call-update
  46.0 0.0 reduce-scatter.5.cloned.1.call-start
  46.0 81.2 %all-gather.5.cloned.1.call-done = bf16[768,3328]{1,0:T(8,128)(2,1)} async-done(((bf16[48,3328]{1,0:T(8,128)(2,1)}), bf16[768,3328]{1,0:T(8,128)(2,1)}) %all-gather.5.cloned.1.call-update) | async-done | bytes 5111824 | tf_op jit(solution)/shard_map/all_gather | solution.py:11
  127.2 10.2 %fusion.19 = f32[768,1024]{1,0:T(8,128)} fusion(bf16[768,3328]{1,0:T(8,128)(2,1)} %all-gather.5.cloned.1.call-done, bf16[3328,1024]{1,0:T(8,128)(2,1)} %param.8), kind=kOutput, calls=%fused_computation.35 | convolution fusion | flops 5234491392 | bytes 15073280 | tf_op jit(solution)/shard_map/dot_general | solution.py:51
  137.4 0.0 reduce-scatter.5.cloned.1.call-update
  137.5 0.0 reduce-scatter.9.cloned.1.call-start
  137.5 68.5 %all-gather.9.cloned.1.call-done = bf16[768,2048]{1,0:T(8,128)(2,1)} async-done(((bf16[48,2048]{1,0:T(8,128)(2,1)}), bf16[768,2048]{1,0:T(8,128)(2,1)}) %all-gather.9.cloned.1.call-update) | async-done | bytes 3145744 | tf_op jit(solution)/shard_map/all_gather | solution.py:11
  206.0 8.3 %fusion.21 = f32[768,1024]{1,0:T(8,128)} fusion(bf16[768,2048]{1,0:T(8,128)(2,1)} %all-gather.9.cloned.1.call-done, bf16[1024,2048]{1,0:T(8,128)(2,1)} %param.9), kind=kOutput, calls=%fused_computation.37 | convolution fusion | flops 3221225472 | bytes 10485760 | tf_op jit(solution)/shard_map/dot_general | solution.py:34
  214.2 0.0 reduce-scatter.9.cloned.1.call-update
  214.3 0.0 all-gather.7.cloned.1.call-start
  214.3 31.8 %reduce-scatter.5.cloned.1.call-done = f32[96,1024]{1,0:T(8,128)} async-done(((f32[768,1024]{1,0:T(8,128)}), f32[96,1024]{1,0:T(8,128)}) %reduce-scatter.5.cloned.1.call-update) | async-done | bytes 393232 | tf_op jit(solution)/shard_map/reduce_scatter | solution.py:24
  246.1 1.7 convert_element_type.34
  247.8 0.0 all-gather.7.cloned.1.call-update
  247.8 0.0 all-gather.11.cloned.1.call-start
  247.9 35.6 %reduce-scatter.9.cloned.1.call-done = f32[96,1024]{1,0:T(8,128)} async-done(((f32[768,1024]{1,0:T(8,128)}), f32[96,1024]{1,0:T(8,128)}) %reduce-scatter.9.cloned.1.call-update) | async-done | bytes 393232 | tf_op jit(solution)/shard_map/reduce_scatter | solution.py:24
  283.5 1.7 convert_element_type.40
  285.2 0.0 all-gather.11.cloned.1.call-update
  285.2 0.0 reduce-scatter.7.cloned.1.call-start
  285.3 27.0 %all-gather.7.cloned.1.call-done = bf16[768,1024]{1,0:T(8,128)(2,1)} async-done(((bf16[96,1024]{1,0:T(8,128)(2,1)}), bf16[768,1024]{1,0:T(8,128)(2,1)}) %all-gather.7.cloned.1.call-update) | async-done | bytes 1572880 | tf_op jit(solution)/shard_map/all_gather | solution.py:30
  312.3 8.7 %fusion.20 = f32[768,2048]{1,0:T(8,128)} fusion(bf16[768,1024]{1,0:T(8,128)(2,1)} %all-gather.7.cloned.1.call-done, bf16[1024,2048]{1,0:T(8,128)(2,1)} %param.9), kind=kOutput, calls=%fused_computation.36 | convolution fusion | flops 3221225472 | bytes 12058624 | tf_op jit(solution)/shard_map/dot_general | solution.py:56
  321.0 0.0 reduce-scatter.7.cloned.1.call-update
  321.0 0.2 reduce-scatter.11.cloned.1.call-start
  321.2 17.9 %all-gather.11.cloned.1.call-done = bf16[768,1024]{1,0:T(8,128)(2,1)} async-done(((bf16[96,1024]{1,0:T(8,128)(2,1)}), bf16[768,1024]{1,0:T(8,128)(2,1)}) %all-gather.11.cloned.1.call-update) | async-done | bytes 1572880 | tf_op jit(solution)/shard_map/all_gather | solution.py:30
  339.1 11.2 %fusion.22 = f32[768,3328]{1,0:T(8,128)} fusion(bf16[768,1024]{1,0:T(8,128)(2,1)} %all-gather.11.cloned.1.call-done, bf16[3328,1024]{1,0:T(8,128)(2,1)} %param.8), kind=kOutput, calls=%fused_computation.38 | convolution fusion | flops 5234491392 | bytes 18612224 | tf_op jit(solution)/shard_map/dot_general | solution.py:34
  350.3 0.0 copy-start.1
  350.3 0.0 reduce-scatter.11.cloned.1.call-update
  350.3 1.4 copy-done.1
  351.7 9.9 %fusion = bf16[3328,1024]{0,1:T(8,128)(2,1)} fusion(bf16[768,1024]{1,0:T(8,128)(2,1)S(1)} %copy-done.1, bf16[768,3328]{1,0:T(8,128)(2,1)} %all-gather.5.cloned.1.call-done), kind=kOutput, calls=%fused_computation.1 | convolution fusion | flops 5237899264 | bytes 13500416 | tf_op jit(solution)/shard_map/dot_general | solution.py:40
  361.6 0.0 copy-start
  361.6 10.1 %copy.11 = bf16[3328,1024]{1,0:T(8,128)(2,1)} copy(bf16[3328,1024]{0,1:T(8,128)(2,1)} %fusion) | data formatting | bytes 13631488
  371.7 0.0 copy-done
  371.7 6.4 convolution_convert_fusion.1
  378.2 101.3 %reduce-scatter.7.cloned.1.call-done = f32[48,2048]{1,0:T(8,128)} async-done(((f32[768,2048]{1,0:T(8,128)}), f32[48,2048]{1,0:T(8,128)}) %reduce-scatter.7.cloned.1.call-update) | async-done | bytes 393232 | tf_op jit(solution)/shard_map/reduce_scatter | solution.py:15
  479.5 1.7 convert_element_type.35
  481.2 218.9 %reduce-scatter.11.cloned.1.call-done = f32[48,3328]{1,0:T(8,128)} async-done(((f32[768,3328]{1,0:T(8,128)}), f32[48,3328]{1,0:T(8,128)}) %reduce-scatter.11.cloned.1.call-update) | async-done | bytes 638992 | tf_op jit(solution)/shard_map/reduce_scatter | solution.py:15
  700.1 1.8 convert_element_type.41
Async XLA Ops:
  7.2 120.0 %all-gather.5.cloned.1.call-start = ((), (), s32[]{:S(2)}) async-start(), calls=%async_computation.4 | async-start | bytes 5431296 | tf_op jit(solution)/shard_map/all_gather | solution.py:11
  7.9 198.1 %all-gather.9.cloned.1.call-start = ((), (), s32[]{:S(2)}) async-start(), calls=%async_computation.8 | async-start | bytes 3342336 | tf_op jit(solution)/shard_map/all_gather | solution.py:11
  46.0 200.1 %reduce-scatter.5.cloned.1.call-start = ((), (), s32[]{:S(2)}) async-start(), calls=%async_computation.5 | async-start | bytes 3538944 | tf_op jit(solution)/shard_map/reduce_scatter | solution.py:24
  137.5 146.0 %reduce-scatter.9.cloned.1.call-start = ((), (), s32[]{:S(2)}) async-start(), calls=%async_computation.9 | async-start | bytes 3538944 | tf_op jit(solution)/shard_map/reduce_scatter | solution.py:24
  214.3 98.0 %all-gather.7.cloned.1.call-start = ((), (), s32[]{:S(2)}) async-start(), calls=%async_computation.6 | async-start | bytes 1769472 | tf_op jit(solution)/shard_map/all_gather | solution.py:30
  247.8 91.3 %all-gather.11.cloned.1.call-start = ((), (), s32[]{:S(2)}) async-start(), calls=%async_computation.10 | async-start | bytes 1769472 | tf_op jit(solution)/shard_map/all_gather | solution.py:30
  285.2 194.3 %reduce-scatter.7.cloned.1.call-start = ((), (), s32[]{:S(2)}) async-start(), calls=%async_computation.7 | async-start | bytes 6684672 | tf_op jit(solution)/shard_map/reduce_scatter | solution.py:15
  321.0 379.1 %reduce-scatter.11.cloned.1.call-start = ((), (), s32[]{:S(2)}) async-start(), calls=%async_computation.11 | async-start | bytes 10862592 | tf_op jit(solution)/shard_map/reduce_scatter | solution.py:15
  350.3 1.4 copy-start.1
  361.6 10.1 %copy-start = (bf16[768,2048]{1,0:T(8,128)(2,1)S(1)}, bf16[768,2048]{1,0:T(8,128)(2,1)}, u32[]{:S(2)}) copy-start(bf16[768,2048]{1,0:T(8,128)(2,1)} %all-gather.9.cloned.1.call-done) | copy-start | bytes 9437188
Sparse Core Ops, SparseCore 0:
  9.6 117.5 all-gather.4
  129.4 76.5 all-gather.8
  209.0 37.0 reduce-scatter.4
  248.9 34.5 reduce-scatter.8
  285.6 26.6 all-gather.6
  314.4 24.6 all-gather.10
  341.5 137.9 reduce-scatter.6
  481.9 218.1 reduce-scatter.10
where the time goes:
time: 709 us
  waiting for transfers between devices  583 us (82%)
  matrix products  55.8 us (8%)
  blocking collectives  33.9 us (5%)
  between operations  14.1 us (2%)
  local copies, waits for them, and re-layouts  11.5 us (2%)
  other arithmetic  10 us (1%)
    reduce_scatter x2, waiting for transfers between devices, scatter_rows(): lax.psum_scatter(term(jnp.int32(0), local_rows * lax.axis_size(('ia', 'ka...  320 us
    all_gather x2, waiting for transfers between devices, gather_rows(): return lax.all_gather(block, ('ia', 'ka'), axis=0, tiled=True)  150 us
    reduce_scatter x2, waiting for transfers between devices, summed_middle(): lax.psum_scatter(term(jnp.int32(0), total_rows // lax.axis_size('ja') * l...  67.4 us
    all_gather x2, waiting for transfers between devices, summed_middle(): return lax.all_gather(shares, 'ja', axis=0, tiled=True)  44.8 us
    psum x1, blocking collectives, local(): margin = lax.psum(local_margin, ('ia', 'ka'))  33.9 us
    dot_general x2, matrix products, contract_last(): lax.dot_general(left, right, (((1,), (1,)), ((), ())), preferred_element_...  19.4 us
    dot_general x2, matrix products, contract_first(): lax.dot_general(left, right, (((0,), (0,)), ((), ())), preferred_element_...  16.3 us
  transfers between devices with their start and end apart: 8, of which 8 were waited for; matrix products, arithmetic and copies ran while one was open for 10% of the time, Pallas kernels for 0%

commit v1 on v0

--- a/solution.py
+++ b/solution.py
@@ -8,7 +8,9 @@
 
 
 def gather_rows(block):
-    return lax.all_gather(block, ("ia", "ka"), axis=0, tiled=True)
+    return jnp.concatenate(
+        lax.all_to_all(jnp.stack([block] * lax.axis_size(("ia", "ka"))), ("ia", "ka"), 0, 0), axis=0
+    )
 
 
 def scatter_rows(term, local_rows):

time: 709 us -> 620 us (0.87)
  waiting for transfers between devices: 583 us -> 408 us
  blocking collectives: 33.9 us -> 126 us
    all_gather x2 -> x0, waiting for transfers between devices: 150 us -> none  [gather_rows(): return lax.all_gather(block, ('ia', 'ka'), axis=0, tiled=True)]
    all_to_all x0 -> x2, blocking collectives: none -> 97.9 us  [gather_rows(): lax.all_to_all(jnp.stack([block] * lax.axis_size(('ia', 'ka'))), ('ia', '...]
    reduce_scatter x2, waiting for transfers between devices: 67.4 us -> 41.6 us  [summed_middle(): lax.psum_scatter(term(jnp.int32(0), total_rows // lax.axis_size('ja') * l...]
  transfers between devices with their start and end apart: 8 -> 6, of which waited for: 8 -> 5; matrix products, arithmetic and copies ran while one was open for 10% -> 9% of each run, Pallas kernels for 0% -> 0%
where the time goes in v1:
time: 620 us; the launch traced here: 619 us
  waiting for transfers between devices  408 us (66%)
  blocking collectives  126 us (20%)
  matrix products  49.2 us (8%)
  between operations  14.2 us (2%)
  local copies, waits for them, and re-layouts  14.1 us (2%)
  other arithmetic  7.08 us (1%)
    reduce_scatter x2, waiting for transfers between devices, scatter_rows(): lax.psum_scatter(term(jnp.int32(0), local_rows * lax.axis_size(('ia', 'ka...  321 us
    all_to_all x2, blocking collectives, gather_rows(): lax.all_to_all(jnp.stack([block] * lax.axis_size(('ia', 'ka'))), ('ia', '...  97.9 us
    all_gather x2, waiting for transfers between devices, summed_middle(): return lax.all_gather(shares, 'ja', axis=0, tiled=True)  45 us
    reduce_scatter x2, waiting for transfers between devices, summed_middle(): lax.psum_scatter(term(jnp.int32(0), total_rows // lax.axis_size('ja') * l...  41.6 us
    psum x1, blocking collectives, local(): margin = lax.psum(local_margin, ('ia', 'ka'))  28.4 us
    dot_general x2, matrix products, contract_first(): lax.dot_general(left, right, (((0,), (0,)), ((), ())), preferred_element_...  16.6 us
    dot_general x2, matrix products, contract_last(): lax.dot_general(left, right, (((1,), (1,)), ((), ())), preferred_element_...  16.4 us
  transfers between devices with their start and end apart: 6, of which 5 were waited for; matrix products, arithmetic and copies ran while one was open for 9% of the time, Pallas kernels for 0%

profile of v1, /device:TPU:9, one launch (start us, length us, event | category | flops | bytes accessed | tf_op | source)
XLA Modules:
  0.0 619.2 jit_solution(6847951296326103133)
XLA Ops:
  7.2 0.0 reduce-scatter.5.cloned.1.call-start
  7.2 0.0 slice-start
  7.2 1.4 stack.4
  8.7 0.0 slice-start.1
  8.7 64.8 %all_to_all.10 = bf16[16,48,3328]{2,1,0:T(8,128)(2,1)S(1)} all-to-all(bf16[16,48,3328]{2,1,0:T(8,128)(2,1)S(1)} %stack.4), channel_id=1, replica_groups=mesh['ia'=2,'ja'=8,'ka'=8] {'ia','ka'}, dimensions={0} | all-to-all | bytes 10223616 | tf_op jit(solution)/shard_map/all_to_all | solution.py:12
  73.5 2.3 copy-done
  75.8 0.0 slice-done
  75.9 0.0 slice-done.1
  75.9 0.0 copy-start.3
  75.9 0.0 copy-start.5
  75.9 0.0 copy-start.1
  75.9 7.1 %fusion.19 = f32[768,1024]{1,0:T(8,128)} fusion(bf16[768,3328]{1,0:T(8,128)(2,1)S(1)} %bitcast.28, bf16[3328,1024]{1,0:T(8,128)(2,1)S(1)} %bitcast.33), kind=kOutput, calls=%fused_computation.35 | convolution fusion | flops 5234491392 | bytes 15073280 | tf_op jit(solution)/shard_map/dot_general | solution.py:53
  83.0 0.0 reduce-scatter.5.cloned.1.call-update
  83.0 0.0 reduce-scatter.9.cloned.1.call-start
  83.1 0.0 copy-done.4
  83.1 0.0 copy-done.3
  83.1 0.2 convolution_bitcast_fusion.1
  83.3 28.4 %psum.7 = f32[8]{0:T(128)S(1)} all-reduce(f32[8]{0:T(128)S(1)} %convolution_bitcast_fusion.1), channel_id=1, replica_groups=mesh['ia'=2,'ja'=8,'ka'=8] {'ia','ka'}, use_global_device_ids=true, to_apply=%region_2.3 | all-reduce | flops 8 | bytes 64 | tf_op jit(solution)/shard_map/psum | solution.py:67
  111.7 0.2 fusion.1
  111.9 0.1 multiply_convert_fusion
  112.0 0.0 copy-start.2
  112.1 0.4 stack.5
  112.4 33.0 %all_to_all.11 = bf16[16,48,2048]{2,1,0:T(8,128)(2,1)S(1)} all-to-all(bf16[16,48,2048]{2,1,0:T(8,128)(2,1)S(1)} %stack.5), channel_id=1, replica_groups=mesh['ia'=2,'ja'=8,'ka'=8] {'ia','ka'}, dimensions={0} | all-to-all | bytes 6291456 | tf_op jit(solution)/shard_map/all_to_all | solution.py:12
  145.5 5.2 fusion.21
  150.7 0.0 reduce-scatter.9.cloned.1.call-update
  150.7 0.0 all-gather.3.cloned.1.call-start
  150.7 0.0 reduce-scatter.5.cloned.1.call-done
  150.8 1.7 convert_element_type.34
  152.5 0.0 all-gather.3.cloned.1.call-update
  152.5 0.0 all-gather.5.cloned.1.call-start
  152.5 41.6 %reduce-scatter.9.cloned.1.call-done = f32[96,1024]{1,0:T(8,128)} async-done(((f32[768,1024]{1,0:T(8,128)}), f32[96,1024]{1,0:T(8,128)}) %reduce-scatter.9.cloned.1.call-update) | async-done | bytes 393232 | tf_op jit(solution)/shard_map/reduce_scatter | solution.py:26
  194.1 1.7 convert_element_type.40
  195.8 0.0 all-gather.5.cloned.1.call-update
  195.8 0.0 reduce-scatter.7.cloned.1.call-start
  195.9 27.1 %all-gather.3.cloned.1.call-done = bf16[768,1024]{1,0:T(8,128)(2,1)} async-done(((bf16[96,1024]{1,0:T(8,128)(2,1)}), bf16[768,1024]{1,0:T(8,128)(2,1)}) %all-gather.3.cloned.1.call-update) | async-done | bytes 1572880 | tf_op jit(solution)/shard_map/all_gather | solution.py:32
  223.0 8.7 %fusion.20 = f32[768,2048]{1,0:T(8,128)} fusion(bf16[768,1024]{1,0:T(8,128)(2,1)} %all-gather.3.cloned.1.call-done, bf16[1024,2048]{1,0:T(8,128)(2,1)} %param.9), kind=kOutput, calls=%fused_computation.36 | convolution fusion | flops 3221225472 | bytes 12058624 | tf_op jit(solution)/shard_map/dot_general | solution.py:58
  231.7 0.0 reduce-scatter.7.cloned.1.call-update
  231.7 0.2 reduce-scatter.11.cloned.1.call-start
  232.0 17.9 %all-gather.5.cloned.1.call-done = bf16[768,1024]{1,0:T(8,128)(2,1)} async-done(((bf16[96,1024]{1,0:T(8,128)(2,1)}), bf16[768,1024]{1,0:T(8,128)(2,1)}) %all-gather.5.cloned.1.call-update) | async-done | bytes 1572880 | tf_op jit(solution)/shard_map/all_gather | solution.py:32
  249.8 11.2 %fusion.22 = f32[768,3328]{1,0:T(8,128)} fusion(bf16[768,1024]{1,0:T(8,128)(2,1)} %all-gather.5.cloned.1.call-done, bf16[3328,1024]{1,0:T(8,128)(2,1)} %param.8), kind=kOutput, calls=%fused_computation.38 | convolution fusion | flops 5234491392 | bytes 18612224 | tf_op jit(solution)/shard_map/dot_general | solution.py:36
  261.0 0.0 reduce-scatter.11.cloned.1.call-update
  261.1 10.2 %fusion = bf16[3328,1024]{0,1:T(8,128)(2,1)} fusion(bf16[768,1024]{1,0:T(8,128)(2,1)} %all-gather.5.cloned.1.call-done, bf16[768,3328]{1,0:T(8,128)(2,1)} %bitcast.29), kind=kOutput, calls=%fused_computation.1 | convolution fusion | flops 5237899264 | bytes 13500416 | tf_op jit(solution)/shard_map/dot_general | solution.py:42
  271.2 9.9 %copy.11 = bf16[3328,1024]{1,0:T(8,128)(2,1)} copy(bf16[3328,1024]{0,1:T(8,128)(2,1)} %fusion) | data formatting | bytes 13631488
  281.2 6.4 %convolution_convert_fusion.1 = bf16[1024,2048]{1,0:T(8,128)(2,1)} fusion(bf16[768,1024]{1,0:T(8,128)(2,1)} %all-gather.3.cloned.1.call-done, bf16[768,2048]{1,0:T(8,128)(2,1)S(1)} %bitcast.31), kind=kOutput, calls=%fused_computation.2 | convolution fusion | flops 3223322624 | bytes 8912896 | tf_op jit(solution)/shard_map/dot_general | solution.py:42
  287.6 102.3 %reduce-scatter.7.cloned.1.call-done = f32[48,2048]{1,0:T(8,128)} async-done(((f32[768,2048]{1,0:T(8,128)}), f32[48,2048]{1,0:T(8,128)}) %reduce-scatter.7.cloned.1.call-update) | async-done | bytes 393232 | tf_op jit(solution)/shard_map/reduce_scatter | solution.py:17
  389.9 1.7 convert_element_type.35
  391.6 218.9 %reduce-scatter.11.cloned.1.call-done = f32[48,3328]{1,0:T(8,128)} async-done(((f32[768,3328]{1,0:T(8,128)}), f32[48,3328]{1,0:T(8,128)}) %reduce-scatter.11.cloned.1.call-update) | async-done | bytes 638992 | tf_op jit(solution)/shard_map/reduce_scatter | solution.py:17
  610.5 1.8 convert_element_type.41
  (8 shorter events, 0.0 us)
Async XLA Ops:
  7.2 143.6 %reduce-scatter.5.cloned.1.call-start = ((), (), s32[]{:S(2)}) async-start(), calls=%async_computation.6 | async-start | bytes 3538944 | tf_op jit(solution)/shard_map/reduce_scatter | solution.py:26
  7.2 68.6 %slice-start = ((s8[6815744]{0:T(1024)(128)(4,1)}), s8[4194304]{0:T(1024)(128)(4,1)S(1)}, s32[]{:S(2)}) async-start(s8[6815744]{0:T(1024)(128)(4,1)} %bitcast.32), calls=%async_computation.12 | async-start | bytes 8388608
  8.7 67.2 %slice-start.1 = ((s8[6815744]{0:T(1024)(128)(4,1)}), s8[2621440]{0:T(1024)(128)(4,1)S(1)}, s32[]{:S(2)}) async-start(s8[6815744]{0:T(1024)(128)(4,1)} %bitcast.32), calls=%async_computation.13 | async-start | bytes 5242880
  73.5 2.3 copy-start
  75.9 7.2 %copy-start.4 = (s32[48]{0:T(128)S(1)}, s32[48]{0:T(128)}, u32[]{:S(2)}) copy-start(s32[48]{0:T(128)} %param.12) | copy-start | bytes 580
  75.9 7.2 %copy-start.3 = (s32[48]{0:T(128)S(1)}, s32[48]{0:T(128)}, u32[]{:S(2)}) copy-start(s32[48]{0:T(128)} %param.13) | copy-start | bytes 580
  75.9 7.2 %copy-start.5 = (f32[48]{0:T(128)S(1)}, f32[48]{0:T(128)}, u32[]{:S(2)}) copy-start(f32[48]{0:T(128)} %param.11) | copy-start | bytes 580
  75.9 36.0 %copy-start.1 = (bf16[48,2048]{1,0:T(8,128)(2,1)S(1)}, bf16[48,2048]{1,0:T(8,128)(2,1)}, u32[]{:S(2)}) copy-start(bf16[48,2048]{1,0:T(8,128)(2,1)} %param.10) | copy-start | bytes 589828
  83.0 111.1 %reduce-scatter.9.cloned.1.call-start = ((), (), s32[]{:S(2)}) async-start(), calls=%async_computation.9 | async-start | bytes 3538944 | tf_op jit(solution)/shard_map/reduce_scatter | solution.py:26
  112.0 33.4 %copy-start.2 = (bf16[1024,2048]{1,0:T(8,128)(2,1)S(1)}, bf16[1024,2048]{1,0:T(8,128)(2,1)}, u32[]{:S(2)}) copy-start(bf16[1024,2048]{1,0:T(8,128)(2,1)} %param.9) | copy-start | bytes 12582916
  150.7 72.3 %all-gather.3.cloned.1.call-start = ((), (), s32[]{:S(2)}) async-start(), calls=%async_computation.7 | async-start | bytes 1769472 | tf_op jit(solution)/shard_map/all_gather | solution.py:32
  152.5 97.3 %all-gather.5.cloned.1.call-start = ((), (), s32[]{:S(2)}) async-start(), calls=%async_computation.10 | async-start | bytes 1769472 | tf_op jit(solution)/shard_map/all_gather | solution.py:32
  195.8 194.1 %reduce-scatter.7.cloned.1.call-start = ((), (), s32[]{:S(2)}) async-start(), calls=%async_computation.8 | async-start | bytes 6684672 | tf_op jit(solution)/shard_map/reduce_scatter | solution.py:17
  231.7 378.8 %reduce-scatter.11.cloned.1.call-start = ((), (), s32[]{:S(2)}) async-start(), calls=%async_computation.11 | async-start | bytes 10862592 | tf_op jit(solution)/shard_map/reduce_scatter | solution.py:17
Sparse Core Ops, SparseCore 0:
  83.1 34.2 reduce-scatter.4
  150.8 43.2 reduce-scatter.8
  196.4 26.5 all-gather.2
  225.1 24.6 all-gather.4
  252.1 137.8 reduce-scatter.6
  392.2 218.2 reduce-scatter.10
